TPU v7x, 32 devices: a whole 2x2x4 slice. The times are simulated.
32 devices in a mesh: pitch: 4 (over y, x), span: 8 (over z, core).
Axes of the slice: x: 2, y: 2, z: 4, core: 2. Of those that a mesh axis runs over, the one named last changes fastest.
Arguments:
- flow_state: float32 [4, 128, 512, 128], P(None, 'span', 'pitch'), may hold values from -0.36 to 3.4, as said below
- node_offset: float32 [2, 128, 512, 128], P(None, 'span', 'pitch'), may hold values from -0.1 to 0.1
- blade_mode: float32 [2, 128, 128], P(None, 'span'), may hold values from -0.2 to 0.2
- phase_angles: float32 [2], replicated, may hold values from -3.140625 to 3.140625
- lag_series: float32 [2, 3, 2, 4, 128, 128], P(None, None, None, None, 'span'), may hold values from -0.3 to 0.3, as said below
Outputs:
- new_state: float32 [4, 128, 512, 128], P(None, 'span', 'pitch')
- moved_offset: float32 [2, 128, 512, 128], P(None, 'span', 'pitch')
Inputs may be any that keep to these rules, and one draw needn't show every extreme that they name: `flow_state`: built from density in 0.8 to 1.2, velocity components within 0.3 and pressure in 0.7 to 1.3. `lag_series`: entries for density lie within 0.01.
All inputs are finite; a program needn't handle non-finite values.
Results may differ from a plain program's by a relative error of at most 0.00002.
Values sent between devices are 32-bit elements; how exact they have to be, the bound alone decides.
A program may use at most 192 MiB of HBM per device.

v0:
```python
import jax
import jax.numpy as jnp
from jax import lax
from jax.sharding import PartitionSpec as P

HEAT_RATIO = 1.4
TIME_STEP = 0.25
DAMPING = 0.02
SECTION_WEIGHTS = (0.5, 1.0)


def broadcast(value, axis, root):
    mine = lax.axis_index(axis) == root
    return lax.psum(jnp.where(mine, value, jnp.zeros_like(value)), axis)


def padded_2(block, sides, width):
    for axis, dim in sides:
        count = lax.axis_size(axis)
        forward = [(i, i + 1) for i in range(count - 1)]
        forward.append((count - 1, 0))
        backward = [(target, source) for source, target in forward]
        low = lax.ppermute(
            lax.slice_in_dim(block, block.shape[dim] - width, None, axis=dim), axis, forward
        )
        high = lax.ppermute(lax.slice_in_dim(block, 0, width, axis=dim), axis, backward)
        block = jnp.concatenate([low, block, high], axis=dim)
    return block


def fill_ends(padded, axis_pos, depth, at_first, at_last):
    length = padded.shape[axis_pos]
    inner_first = lax.slice_in_dim(padded, depth, depth + 1, axis=axis_pos)
    inner_second = lax.slice_in_dim(padded, depth + 1, depth + 2, axis=axis_pos)
    inner_last = lax.slice_in_dim(padded, length - depth - 1, length - depth, axis=axis_pos)
    inner_before = lax.slice_in_dim(padded, length - depth - 2, length - depth - 1, axis=axis_pos)
    step_low = inner_first - inner_second
    step_high = inner_last - inner_before
    low_side = jnp.concatenate(
        [inner_first + float(count) * step_low for count in range(depth, 0, -1)], axis=axis_pos
    )
    high_side = jnp.concatenate(
        [inner_last + float(count) * step_high for count in range(1, depth + 1)], axis=axis_pos
    )
    low_side = jnp.where(at_first, low_side, lax.slice_in_dim(padded, 0, depth, axis=axis_pos))
    high_side = jnp.where(
        at_last, high_side, lax.slice_in_dim(padded, length - depth, length, axis=axis_pos)
    )
    return jnp.concatenate(
        [low_side, lax.slice_in_dim(padded, depth, length - depth, axis=axis_pos), high_side],
        axis=axis_pos,
    )


def radial_damping(values, axis_pos):
    count = values.shape[axis_pos]
    first_row = lax.slice_in_dim(values, 0, 1, axis=axis_pos)
    last_row = lax.slice_in_dim(values, count - 1, count, axis=axis_pos)
    extended = jnp.concatenate([first_row, first_row, values, last_row, last_row], axis=axis_pos)
    return (
        lax.slice_in_dim(extended, 4, 4 + count, axis=axis_pos)
        - 4.0 * lax.slice_in_dim(extended, 3, 3 + count, axis=axis_pos)
        + 6.0 * values
        - 4.0 * lax.slice_in_dim(extended, 1, 1 + count, axis=axis_pos)
        + lax.slice_in_dim(extended, 0, count, axis=axis_pos)
    )


def unit_normal(earlier, later):
    along_x = later[0] - earlier[0]
    along_y = 1.0 + later[1] - earlier[1]
    length = jnp.sqrt(along_x * along_x + along_y * along_y)
    return jnp.stack([along_x / length, along_y / length])


def wall_amplitude(shape_mode, angle, blade_mask):
    return (shape_mode[0] * jnp.cos(angle) - shape_mode[1] * jnp.sin(angle)) * blade_mask


def lag_shift(series, phase_now, phase_move):
    series_sum = jnp.zeros(series.shape[2:], jnp.float32)
    for number in range(series.shape[0]):
        harmonic = float(number + 1)
        change_cos = jnp.cos(harmonic * (phase_now + phase_move)) - jnp.cos(harmonic * phase_now)
        change_sin = jnp.sin(harmonic * (phase_now + phase_move)) - jnp.sin(harmonic * phase_now)
        series_sum = series_sum + series[number, 0] * change_cos - series[number, 1] * change_sin
    return series_sum


def metric_terms(offset_x, offset_y):
    x_zeta = 1.0 + (offset_x[2:, 1:-1] - offset_x[:-2, 1:-1]) * 0.5
    x_xi = (offset_x[1:-1, 2:] - offset_x[1:-1, :-2]) * 0.5
    y_xi = 1.0 + (offset_y[1:-1, 2:] - offset_y[1:-1, :-2]) * 0.5
    y_zeta = (offset_y[2:, 1:-1] - offset_y[:-2, 1:-1]) * 0.5
    return (x_zeta, x_xi, y_xi, y_zeta)


def geometry(grid_pad):
    x_zeta, x_xi, y_xi, y_zeta = metric_terms(grid_pad[0], grid_pad[1])
    old_zeta, old_xi, oldy_xi, oldy_zeta = metric_terms(
        grid_pad[0] - grid_pad[2], grid_pad[1] - grid_pad[3]
    )
    volume_new = (x_zeta * y_xi - x_xi * y_zeta)[1:-1, 1:-1]
    volume_old = (old_zeta * oldy_xi - old_xi * oldy_zeta)[1:-1, 1:-1]
    speed_x = grid_pad[2][1:-1, 1:-1] / TIME_STEP
    speed_y = grid_pad[3][1:-1, 1:-1] / TIME_STEP
    first_pitch = -y_zeta
    sweep_pitch = first_pitch * speed_x + x_zeta * speed_y
    second_axial = -x_xi
    sweep_axial = y_xi * speed_x + second_axial * speed_y
    return (
        (first_pitch, x_zeta, sweep_pitch, y_xi, second_axial, sweep_axial),
        volume_old,
        volume_new,
    )


def directional(strip_cells, first_coef, second_coef, sweep_term):
    density = strip_cells[0]
    vel_x = strip_cells[1] / density
    vel_y = strip_cells[2] / density
    energy = strip_cells[3]
    pressure = (HEAT_RATIO - 1.0) * (energy - 0.5 * density * (vel_x * vel_x + vel_y * vel_y))
    flux_x = jnp.stack(
        [
            strip_cells[1],
            strip_cells[1] * vel_x + pressure,
            strip_cells[1] * vel_y,
            (energy + pressure) * vel_x,
        ]
    )
    flux_y = jnp.stack(
        [
            strip_cells[2],
            strip_cells[2] * vel_x,
            strip_cells[2] * vel_y + pressure,
            (energy + pressure) * vel_y,
        ]
    )
    return first_coef * flux_x + second_coef * flux_y - sweep_term * strip_cells


def residual(padded, geo_terms):
    first_pitch, second_pitch, sweep_pitch, first_axial, second_axial, sweep_axial = geo_terms
    pitch_flux = directional(
        padded[:, 2:-2, 1:-1], first_pitch[1:-1], second_pitch[1:-1], sweep_pitch[1:-1]
    )
    axial_flux = directional(
        padded[:, 1:-1, 2:-2], first_axial[:, 1:-1], second_axial[:, 1:-1], sweep_axial[:, 1:-1]
    )
    divergence = (pitch_flux[:, :, 2:] - pitch_flux[:, :, :-2]) * 0.5 + (
        axial_flux[:, 2:] - axial_flux[:, :-2]
    ) * 0.5
    centre = padded[:, 2:-2, 2:-2]
    fourth = (
        padded[:, 2:-2, 4:]
        - 4.0 * padded[:, 2:-2, 3:-1]
        + 6.0 * centre
        - 4.0 * padded[:, 2:-2, 1:-3]
        + padded[:, 2:-2, :-4]
        + (
            padded[:, 4:, 2:-2]
            - 4.0 * padded[:, 3:-1, 2:-2]
            + 6.0 * centre
            - 4.0 * padded[:, 1:-3, 2:-2]
            + padded[:, :-4, 2:-2]
        )
    )
    return divergence + DAMPING * fourth + DAMPING * radial_damping(centre, 3)


def flow_ghosts(
    row_zero,
    row_one,
    row_last,
    row_before,
    wrap_low0,
    wrap_low1,
    wrap_high0,
    wrap_high1,
    blade_flag,
    corr_low,
    corr_high,
):
    sign_flip = jnp.array([1.0, 1.0, -1.0, 1.0], jnp.float32).reshape(
        (4,) + (1,) * (row_zero.ndim - 1)
    )
    ghost_m2 = jnp.where(blade_flag, row_one * sign_flip, wrap_low0 + corr_low)
    ghost_m1 = jnp.where(blade_flag, row_zero * sign_flip, wrap_low1 + corr_low)
    ghost_p0 = jnp.where(blade_flag, row_last * sign_flip, wrap_high0 + corr_high)
    ghost_p1 = jnp.where(blade_flag, row_before * sign_flip, wrap_high1 + corr_high)
    return (ghost_m2, ghost_m1, ghost_p0, ghost_p1)


def finish_flow(
    padded, depth, row_flag, corr_low, corr_high, low_end, high_end, first_end, last_end
):
    middle_rows = padded[:, 2:-2]
    width = middle_rows.shape[2]
    ghost_m2, ghost_m1, ghost_p0, ghost_p1 = flow_ghosts(
        middle_rows[:, :, 2],
        middle_rows[:, :, 3],
        middle_rows[:, :, width - 3],
        middle_rows[:, :, width - 4],
        middle_rows[:, :, 0],
        middle_rows[:, :, 1],
        middle_rows[:, :, width - 2],
        middle_rows[:, :, width - 1],
        row_flag[:, None],
        corr_low,
        corr_high,
    )
    low_pair = jnp.where(low_end, jnp.stack([ghost_m2, ghost_m1], 2), middle_rows[:, :, 0:2])
    high_pair = jnp.where(
        high_end, jnp.stack([ghost_p0, ghost_p1], 2), middle_rows[:, :, width - 2 :]
    )
    middle_rows = jnp.concatenate([low_pair, middle_rows[:, :, 2 : width - 2], high_pair], 2)
    whole = jnp.concatenate([padded[:, 0:2], middle_rows, padded[:, -2:]], 1)
    top_copy = jnp.repeat(whole[:, depth : depth + 1], depth, axis=1)
    bottom_copy = jnp.repeat(whole[:, -depth - 1 : -depth], depth, axis=1)
    top_rows = jnp.where(first_end, top_copy, whole[:, :depth])
    bottom_rows = jnp.where(last_end, bottom_copy, whole[:, -depth:])
    return jnp.concatenate([top_rows, whole[:, depth:-depth], bottom_rows], 1)


def per_device(flow_state, node_offset, blade_mode, phase_angles, lag_series):
    n_pitch = lax.axis_size("pitch")
    n_span = lax.axis_size("span")
    pitch_rows = flow_state.shape[2]
    axial_cols = flow_state.shape[1]
    total_pitch = pitch_rows * n_pitch
    total_axial = axial_cols * n_span
    pitch_at = lax.axis_index("pitch")
    span_at = lax.axis_index("span")
    lead_edge = total_axial // 4
    axial_index = span_at * axial_cols + jnp.arange(axial_cols, dtype=jnp.int32)
    blade_flag = (axial_index >= lead_edge) & (axial_index < total_axial - lead_edge)
    blade_mask = blade_flag.astype(jnp.float32)[:, None]
    phase_now = phase_angles[0]
    phase_lag = phase_angles[1]
    low_guess = wall_amplitude(blade_mode, phase_now, blade_mask) * unit_normal(
        node_offset[:, :, 0], node_offset[:, :, 1]
    )
    high_guess = wall_amplitude(blade_mode, phase_now + phase_lag, blade_mask) * unit_normal(
        node_offset[:, :, pitch_rows - 2], node_offset[:, :, pitch_rows - 1]
    )
    low_wall = broadcast(low_guess, "pitch", 0)
    high_wall = broadcast(high_guess, "pitch", n_pitch - 1)
    pitch_index = pitch_at * pitch_rows + jnp.arange(pitch_rows, dtype=jnp.int32)
    blend_row = (pitch_index.astype(jnp.float32) / (total_pitch - 1))[:, None]
    shift_field = (1.0 - blend_row) * low_wall[:, :, None, :] + blend_row * high_wall[:, :, None, :]
    moved_offset = node_offset + shift_field
    grid_field = jnp.concatenate([moved_offset, shift_field], 0)
    rim_width = 2
    joined = padded_2(
        jnp.concatenate([flow_state, grid_field], 0), (("pitch", 2), ("span", 1)), rim_width
    )
    first_pad = joined[:4]
    grid_pad = joined[4:]
    low_end = pitch_at == 0
    high_end = pitch_at == n_pitch - 1
    first_end = span_at == 0
    last_end = span_at == n_span - 1
    grid_pad = fill_ends(grid_pad, 1, rim_width, first_end, last_end)
    grid_pad = fill_ends(grid_pad, 2, 2, low_end, high_end)
    geo_terms, volume_old, volume_new = geometry(grid_pad)
    corr_low = lag_shift(lag_series[1], phase_now, -phase_lag)
    corr_high = lag_shift(lag_series[0], phase_now, phase_lag)
    padded = finish_flow(
        first_pad, 2, blade_flag, corr_low, corr_high, low_end, high_end, first_end, last_end
    )
    section_one = (
        volume_old * flow_state - SECTION_WEIGHTS[0] * TIME_STEP * residual(padded, geo_terms)
    ) / volume_new
    second_pad = padded_2(section_one, (("pitch", 2), ("span", 1)), 2)
    padded = finish_flow(
        second_pad, 2, blade_flag, corr_low, corr_high, low_end, high_end, first_end, last_end
    )
    current = (
        volume_old * flow_state - SECTION_WEIGHTS[1] * TIME_STEP * residual(padded, geo_terms)
    ) / volume_new
    return (current, moved_offset)


def solution(mesh):
    placed = (
        P(None, "span", "pitch", None),
        P(None, "span", "pitch", None),
        P(None, "span", None),
        P(),
        P(None, None, None, None, "span", None),
    )
    return jax.shard_map(
        per_device,
        mesh=mesh,
        in_specs=placed,
        out_specs=(P(None, "span", "pitch", None), P(None, "span", "pitch", None)),
        check_vma=False,
    )
```

profile of v0, /device:TPU:0, one launch (start us, length us, event | category | flops | bytes accessed | tf_op | source)
XLA Modules:
  0.0 227.0 jit_solution(227940190196218622)
XLA Ops:
  6.8 17.8 %all-reduce = (f32[2,16,128]{2,1,0:T(8,128)S(1)}, f32[2,16,128]{2,1,0:T(8,128)S(1)}) all-reduce(f32[2,16,128]{2,1,0:T(8,128)S(1)} %get-tuple-element.167, f32[2,16,128]{2,1,0:T(8,128)S(1)} %get-tuple-element.166), channel_id=1, replica_groups=mesh['pitch'=4,'span'=8] {'pitch'}, use_global_device_ids=true, to_apply=%region_1.2 | all-reduce | flops 8192 | bytes 65536 | tf_op jit(solution)/shard_map/psum | solution.py:14
  24.6 2.2 fusion.90
  28.2 2.9 %collective-permute-start.1 = (f32[8,16,2,128]{3,2,1,0:T(2,128)S(1)}, f32[8,16,2,128]{3,2,1,0:T(2,128)S(1)}, u32[]{:S(2)}, u32[]{:S(2)}) collective-permute-start(f32[8,16,2,128]{3,2,1,0:T(2,128)S(1)} %get-tuple-element.56), channel_id=1, source_target_pairs={{8,0},{16,8},{24,16},{0,24},{9,1},{17,9},{25,17},{1,25},{10,2},{18... | collective-permute-start | bytes 393224 | tf_op jit(solution)/shard_map/ppermute | solution.py:26
  34.7 8.2 %fusion.126 = (f32[4,16,128,1]{3,2,1,0:T(8,128)}, f32[4,16,128,1]{3,2,1,0:T(8,128)}) fusion(f32[4,16,128,128]{3,2,1,0:T(8,128)} %param.7), kind=kLoop, calls=%fused_computation.311 | loop fusion | bytes 131072 | tf_op jit(solution)/shard_map/slice | solution.py:58
  47.3 3.5 %collective-permute-start.3 = (f32[8,2,132,128]{3,0,2,1:T(8,128)}, f32[8,2,132,128]{3,0,2,1:T(8,128)}, u32[]{:S(2)}, u32[]{:S(2)}) collective-permute-start(f32[8,2,132,128]{3,0,2,1:T(8,128)} %copy.142), channel_id=1, source_target_pairs={{1,0},{2,1},{3,2},{4,3},{5,4},{6,5},{7,6},{0,7},{9,8},{10,9},{11,1... | collective-permute-start | bytes 3244040 | tf_op jit(solution)/shard_map/ppermute | solution.py:26
  53.3 1.8 copy-done.7
  57.0 2.4 %slice.792 = f32[4,16,132,128]{3,2,1,0:T(8,128)} slice(f32[8,16,132,128]{3,2,1,0:T(8,128)S(1)} %pad_maximum_fusion), slice={[4:8], [0:16], [0:132], [0:128]} | slice | bytes 8650752 | tf_op jit(solution)/shard_map/slice | solution.py:50
  59.4 2.4 %multiply_add_fusion.9 = (f32[1,16,130,128]{3,2,1,0:T(8,128)}, f32[1,16,130,128]{3,2,1,0:T(8,128)S(1)}, f32[1,16,130,128]{3,2,1,0:T(8,128)S(1)}, f32[1,16,130,128]{3,2,1,0:T(8,128)}, f32[1,16,130,128]{3,2,1,0:T(8,128)}) fusion(f32[4,16,132,128]{3,2,1,0:T(8,128)S(1)} %pad_maximum_fusion.7, f32[1,16,130,128]{3,2,1,0:T(8,128)S(1)} %get-tuple-element.19), kind=kLoop, calls=%fused_computation.154 | loop fusion | flops 2662400 | bytes 10649600 | tf_op jit(solution)/shard_map/add | solution.py:136
  62.7 2.4 %multiply_add_fusion.10 = (f32[1,16,130,128]{3,2,1,0:T(8,128)}, f32[1,16,130,128]{3,2,1,0:T(8,128)}, f32[1,16,130,128]{3,2,1,0:T(8,128)}, f32[1,16,130,128]{3,2,1,0:T(8,128)}) fusion(f32[1,16,130,128]{3,2,1,0:T(8,128)S(1)} %get-tuple-element.21, f32[1,16,130,128]{3,2,1,0:T(8,128)S(1)} %get-tuple-element.19, f32[4,16,132,128]{3,2,1,0:T(8,128)S(1)} %pad_maximum_fusion.7, ...), kind=kLoop, calls=%fused_computation.156 | loop fusion | flops 1597440 | bytes 9584640 | tf_op jit(solution)/shard_map/add | solution.py:127
  65.1 5.5 %collective-permute-done.2 = f32[8,2,132,128]{3,0,2,1:T(8,128)} collective-permute-done((f32[8,2,132,128]{3,0,2,1:T(8,128)}, f32[8,2,132,128]{3,0,2,1:T(8,128)}, u32[]{:S(2)}, u32[]{:S(2)}) %collective-permute-start.2) | collective-permute-done | bytes 1081376 | tf_op jit(solution)/shard_map/ppermute | solution.py:23
  70.6 1.8 fusion.132
  72.5 2.7 %fusion.133 = (f32[4,2,132,128]{3,0,2,1:T(4,128)S(1)}, f32[4,2,132,128]{3,0,2,1:T(4,128)}) fusion(f32[8,2,132,128]{3,0,2,1:T(8,128)} %collective-permute-done.3), kind=kLoop, calls=%fused_computation.318 | loop fusion | bytes 2162688 | tf_op jit(solution)/shard_map/slice | solution.py:47
  75.3 9.1 %pad_maximum_fusion.1 = (f32[4,20,132,128]{3,2,1,0:T(8,128)}, f32[4,20,132,128]{3,2,1,0:T(8,128)}, f32[4,20,132,128]{3,2,1,0:T(8,128)}) fusion(f32[4,2,132,128]{3,2,1,0:T(8,128)S(1)} %maximum_select_fusion.1, f32[4,16,132,128]{3,2,1,0:T(8,128)} %slice.792, f32[4,2,132,128]{3,2,1,0:T(8,128)S(1)} %maximum_select_fusion), kind=kLoop, calls=%fused_computation.1 | loop fusion | flops 2703360 | bytes 21626880 | tf_op jit(solution)/shard_map/concatenate | solution.py:49
  84.3 3.6 %slice.794 = f32[4,20,128,128]{3,2,1,0:T(8,128)S(1)} slice(f32[4,20,132,128]{3,2,1,0:T(8,128)} %get-tuple-element.94), slice={[0:4], [0:20], [2:130], [0:128]} | slice | bytes 10485760 | tf_op jit(solution)/shard_map/slice | solution.py:50
  94.3 4.5 %pad_maximum_fusion.5 = (f32[4,18,132,128]{3,2,1,0:T(8,128)}, f32[4,18,132,128]{3,2,1,0:T(8,128)}) fusion(f32[4,2,132,128]{3,2,1,0:T(8,128)S(1)} %copy_select_fusion, f32[4,16,2,128]{3,2,1,0:T(2,128)S(1)} %slice_select_fusion, f32[4,16,128,128]{3,2,1,0:T(8,128)S(1)} %copy-done.2, f32[4,16,2,128]{3,2,1,0:T(2,128)S(1)} %slice_select_fusion.1, ...), kind=kLoop, calls=%fused_computation.5 | loop fusion | flops 7299072 | bytes 15138816 | tf_op jit(solution)/shard_map/concatenate | solution.py:223
  98.9 2.3 %fusion.128 = (f32[18,130,128]{2,1,0:T(8,128)}, f32[18,130,128]{2,1,0:T(8,128)}, f32[18,130,128]{2,1,0:T(8,128)}, f32[18,130,128]{2,1,0:T(8,128)}) fusion(f32[20,132,128]{2,1,0:T(8,128)S(1)} %get-tuple-element.72), kind=kLoop, calls=%fused_computation.313 | loop fusion | bytes 9584640 | tf_op jit(solution)/shard_map/slice | solution.py:91
  101.2 2.3 %fusion.129 = (f32[18,130,128]{2,1,0:T(8,128)}, f32[18,130,128]{2,1,0:T(8,128)}, f32[18,130,128]{2,1,0:T(8,128)}, f32[18,130,128]{2,1,0:T(8,128)}) fusion(f32[20,132,128]{2,1,0:T(8,128)S(1)} %get-tuple-element.73), kind=kLoop, calls=%fused_computation.314 | loop fusion | bytes 9584640 | tf_op jit(solution)/shard_map/slice | solution.py:93
  106.1 2.1 multiply_add_fusion.5
  112.2 3.2 %multiply_add_fusion.6 = (f32[1,18,128,128]{3,2,1,0:T(8,128)S(1)}, f32[1,18,128,128]{3,2,1,0:T(8,128)S(1)}, f32[1,18,128,128]{3,2,1,0:T(8,128)S(1)}, f32[1,18,128,128]{3,2,1,0:T(8,128)}) fusion(f32[1,18,128,128]{3,2,1,0:T(8,128)S(1)} %copy-done.17, f32[1,18,128,128]{3,2,1,0:T(8,128)S(1)} %get-tuple-element.42, ...), kind=kLoop, calls=%fused_computation.145 | loop fusion | flops 1769472 | bytes 10616832 | tf_op jit(solution)/shard_map/add | solution.py:127
  115.4 5.5 %fusion.75 = f32[16,128,128]{2,1,0:T(8,128)} fusion(f32[18,130,128]{2,1,0:T(8,128)} %get-tuple-element.134, f32[18,130,128]{2,1,0:T(8,128)} %get-tuple-element.135, f32[18,130,128]{2,1,0:T(8,128)} %get-tuple-element.130, f32[18,130,128]{2,1,0:T(8,128)} %get-tuple-element.131, f32[18,130,128]{2,1,0:T(8,128)} %get-tuple-element.136, ...), kind=kLoop, calls=%fused_computation.165 | loop fusion | flops 3407872 | bytes 9437184 | tf_op jit(solution)/shard_map/sub | solution.py:104
  121.0 5.7 %fusion.5 = f32[4,16,130,128]{3,2,1,0:T(8,128)} fusion(f32[4,16,132,128]{3,2,1,0:T(8,128)S(1)} %bitcast.76, f32[1,16,130,128]{3,2,1,0:T(8,128)} %get-tuple-element.67, f32[1,16,130,128]{3,2,1,0:T(8,128)} %get-tuple-element.93, f32[1,16,130,128]{3,2,1,0:T(8,128)} %get-tuple-element.66, f32[1,16,130,128]{3,2,1,0:T(8,128)} %get-tuple-element.92, ...), kind=kLoop, calls=%fused_computation.22 | loop fusion | flops 11714560 | bytes 20234240 | tf_op jit(solution)/shard_map/sub | solution.py:140
  126.7 3.5 %fusion.1 = f32[4,18,128,128]{3,2,1,0:T(8,128)} fusion(f32[4,20,132,128]{3,2,1,0:T(8,128)S(1)} %pad_maximum_fusion.3, f32[1,18,128,128]{3,2,1,0:T(8,128)S(1)} %get-tuple-element.61, f32[1,18,128,128]{3,2,1,0:T(8,128)S(1)} %copy-done.16, f32[1,18,128,128]{3,2,1,0:T(8,128)S(1)} %get-tuple-element.60, f32[1,18,128,128]{3,2,1,0:T(8,128)S(1)} %get-tuple-element.82, ...), kind=kLoop, calls=%fused_computation.12 | loop fusion | flops 12976128 | bytes 22413312 | tf_op jit(solution)/shard_map/sub | solution.py:140
  130.2 21.3 %fusion.32 = f32[4,16,128,128]{3,2,1,0:T(8,128)} fusion(f32[4,16,2,128]{3,2,1,0:T(2,128)S(1)} %slice_select_fusion.1, f32[4,16,128,128]{3,2,1,0:T(8,128)S(1)} %copy-done.2, f32[4,16,2,128]{3,2,1,0:T(2,128)S(1)} %slice_select_fusion, f32[4,16,128,1]{3,2,1,0:T(8,128)} %get-tuple-element.121, f32[4,16,128,1]{3,2,1,0:T(8,128)} %get-tuple-element.120, ...), kind=kLoop, calls=%fused_computation.64 | loop fusion | flops 44040192 | bytes 44236800 | tf_op jit(solution)/shard_map/div | solution.py:272
  152.7 2.9 %collective-permute-start.5 = (f32[4,16,2,128]{3,2,1,0:T(2,128)S(1)}, f32[4,16,2,128]{3,2,1,0:T(2,128)S(1)}, u32[]{:S(2)}, u32[]{:S(2)}) collective-permute-start(f32[4,16,2,128]{3,2,1,0:T(2,128)S(1)} %get-tuple-element.118), channel_id=1, source_target_pairs={{8,0},{16,8},{24,16},{0,24},{9,1},{17,9},{25,17},{1,25},{10,2},{18... | collective-permute-start | bytes 196616 | tf_op jit(solution)/shard_map/ppermute | solution.py:26
  155.6 8.1 %fusion.124 = (f32[4,16,128,1]{3,2,1,0:T(8,128)}, f32[4,16,128,1]{3,2,1,0:T(8,128)}) fusion(f32[4,16,128,128]{3,2,1,0:T(8,128)} %fusion.32), kind=kLoop, calls=%fused_computation.309 | loop fusion | bytes 131072 | tf_op jit(solution)/shard_map/slice | solution.py:58
  165.5 1.8 multiply_add_fusion.7
  168.9 2.6 %collective-permute-start.7 = (f32[4,2,132,128]{3,0,2,1:T(4,128)S(1)}, f32[4,2,132,128]{3,0,2,1:T(4,128)S(1)}, u32[]{:S(2)}, u32[]{:S(2)}) collective-permute-start(f32[4,2,132,128]{3,0,2,1:T(4,128)S(1)} %copy.148), channel_id=1, source_target_pairs={{1,0},{2,1},{3,2},{4,3},{5,4},{6,5},{7,6},{0,7},{9,8},{10,9},{11,1... | collective-permute-start | bytes 1622024 | tf_op jit(solution)/shard_map/ppermute | solution.py:26
  173.4 2.8 %fusion.4 = f32[4,16,130,128]{3,2,1,0:T(8,128)} fusion(f32[4,16,132,128]{3,2,1,0:T(8,128)S(1)} %get-tuple-element.114, f32[1,16,130,128]{3,2,1,0:T(8,128)S(1)} %get-tuple-element.65, f32[1,16,130,128]{3,2,1,0:T(8,128)S(1)} %get-tuple-element.86, f32[1,16,130,128]{3,2,1,0:T(8,128)S(1)} %get-tuple-element.64, f32[1,16,130,128]{3,2,1,0:T(8,128)S(1)} %get-tuple-element.85, ...), kind=kLoop, calls=%fused_computation.20 | loop fusion | flops 11714560 | bytes 20234240 | tf_op jit(solution)/shard_map/sub | solution.py:140
  176.2 3.6 %collective-permute-done.6 = f32[4,2,132,128]{3,0,2,1:T(4,128)S(1)} collective-permute-done((f32[4,2,132,128]{3,0,2,1:T(4,128)S(1)}, f32[4,2,132,128]{3,0,2,1:T(4,128)S(1)}, u32[]{:S(2)}, u32[]{:S(2)}) %collective-permute-start.6) | collective-permute-done | bytes 540704 | tf_op jit(solution)/shard_map/ppermute | solution.py:23
  181.8 4.5 %pad_maximum_fusion.6 = (f32[4,18,132,128]{3,2,1,0:T(8,128)}, f32[4,18,132,128]{3,2,1,0:T(8,128)}) fusion(f32[4,2,132,128]{3,2,1,0:T(8,128)S(1)} %copy_select_fusion.2, f32[4,16,2,128]{3,2,1,0:T(2,128)S(1)} %maximum_select_fusion.5, f32[4,16,128,128]{3,2,1,0:T(8,128)S(1)} %copy-done.3, f32[4,16,2,128]{3,2,1,0:T(2,128)S(1)} %maximum_select_fusion.4, ...), kind=kLoop, calls=%fused_computation.7 | loop fusion | flops 7299072 | bytes 15138816 | tf_op jit(solution)/shard_map/concatenate | solution.py:223
  188.9 3.4 %fusion = f32[4,18,128,128]{3,2,1,0:T(8,128)} fusion(f32[4,20,132,128]{3,2,1,0:T(8,128)S(1)} %pad_maximum_fusion.4, f32[1,18,128,128]{3,2,1,0:T(8,128)S(1)} %get-tuple-element.59, f32[1,18,128,128]{3,2,1,0:T(8,128)S(1)} %get-tuple-element.71, f32[1,18,128,128]{3,2,1,0:T(8,128)S(1)} %get-tuple-element.58, f32[1,18,128,128]{3,2,1,0:T(8,128)S(1)} %get-tuple-element.70, ...), kind=kLoop, calls=%fused_computation.10 | loop fusion | flops 12976128 | bytes 22413312 | tf_op jit(solution)/shard_map/sub | solution.py:140
  192.3 34.6 %fusion.18 = f32[4,16,128,128]{3,2,1,0:T(8,128)} fusion(f32[4,16,2,128]{3,2,1,0:T(2,128)S(1)} %maximum_select_fusion.4, f32[4,16,128,128]{3,2,1,0:T(8,128)} %fusion.32, f32[4,16,2,128]{3,2,1,0:T(2,128)S(1)} %maximum_select_fusion.5, f32[4,16,128,1]{3,2,1,0:T(8,128)} %get-tuple-element.117, f32[4,16,128,1]{3,2,1,0:T(8,128)} %get-tuple-element.116, ...), kind=kLoop, calls=%fused_computation.50 | loop fusion | flops 44040192 | bytes 48431104 | tf_op jit(solution)/shard_map/div | solution.py:279
  (131 shorter events, 38.1 us)
Async XLA Ops:
  24.5 2.8 %copy-start = (f32[4,16,128,128]{3,2,1,0:T(8,128)S(1)}, f32[4,16,128,128]{3,2,1,0:T(8,128)}, u32[]{:S(2)}) copy-start(f32[4,16,128,128]{3,2,1,0:T(8,128)} %param.7) | copy-start | bytes 12582916
  26.8 1.4 copy-start.6
  26.8 28.5 %copy-start.5 = (f32[2,16,128,128]{3,2,1,0:T(8,128)}, f32[2,16,128,128]{3,2,1,0:T(8,128)S(1)}, u32[]{:S(2)}) copy-start(f32[2,16,128,128]{3,2,1,0:T(8,128)S(1)} %get-tuple-element.156) | copy-start | bytes 6291460
  28.1 14.9 %collective-permute-start = (f32[8,16,2,128]{3,2,1,0:T(2,128)S(1)}, f32[8,16,2,128]{3,2,1,0:T(2,128)S(1)}, u32[]{:S(2)}, u32[]{:S(2)}) collective-permute-start(f32[8,16,2,128]{3,2,1,0:T(2,128)S(1)} %get-tuple-element.57), channel_id=1, source_target_pairs={{0,8},{8,16},{16,24},{24,0},{1,9},{9,17},{17,25},{25,1},{2,10},{10... | collective-permute-start | bytes 393224 | tf_op jit(solution)/shard_map/ppermute | solution.py:23
  28.2 14.9 %collective-permute-start.1 = (f32[8,16,2,128]{3,2,1,0:T(2,128)S(1)}, f32[8,16,2,128]{3,2,1,0:T(2,128)S(1)}, u32[]{:S(2)}, u32[]{:S(2)}) collective-permute-start(f32[8,16,2,128]{3,2,1,0:T(2,128)S(1)} %get-tuple-element.56), channel_id=1, source_target_pairs={{8,0},{16,8},{24,16},{0,24},{9,1},{17,9},{25,17},{1,25},{10,2},{18... | collective-permute-start | bytes 393224 | tf_op jit(solution)/shard_map/ppermute | solution.py:26
  34.7 8.2 %copy-start.23 = (f32[2,3,2,4,16,128]{5,4,3,2,1,0:T(8,128)S(1)}, f32[2,3,2,4,16,128]{5,4,3,2,1,0:T(8,128)}, u32[]{:S(2)}) copy-start(f32[2,3,2,4,16,128]{5,4,3,2,1,0:T(8,128)} %param.11) | copy-start | bytes 1179652
  44.6 6.3 %copy-start.1 = (f32[4,16,128,128]{3,2,1,0:T(8,128)S(1)}, f32[4,16,128,128]{3,2,1,0:T(8,128)}, u32[]{:S(2)}) copy-start(f32[4,16,128,128]{3,2,1,0:T(8,128)} %param.7) | copy-start | bytes 12582916
  44.6 6.3 %copy-start.24 = (f32[4]{0:T(128)S(1)}, f32[4]{0:T(128)}, u32[]{:S(2)}) copy-start(f32[4]{0:T(128)} %constant.18.clone) | copy-start | bytes 52
  45.9 24.7 %collective-permute-start.2 = (f32[8,2,132,128]{3,0,2,1:T(8,128)}, f32[8,2,132,128]{3,0,2,1:T(8,128)}, u32[]{:S(2)}, u32[]{:S(2)}) collective-permute-start(f32[8,2,132,128]{3,0,2,1:T(8,128)} %copy.140), channel_id=1, source_target_pairs={{0,1},{1,2},{2,3},{3,4},{4,5},{5,6},{6,7},{7,0},{8,9},{9,10},{10,1... | collective-permute-start | bytes 3244040 | tf_op jit(solution)/shard_map/ppermute | solution.py:23
  47.3 25.1 %collective-permute-start.3 = (f32[8,2,132,128]{3,0,2,1:T(8,128)}, f32[8,2,132,128]{3,0,2,1:T(8,128)}, u32[]{:S(2)}, u32[]{:S(2)}) collective-permute-start(f32[8,2,132,128]{3,0,2,1:T(8,128)} %copy.142), channel_id=1, source_target_pairs={{1,0},{2,1},{3,2},{4,3},{5,4},{6,5},{7,6},{0,7},{9,8},{10,9},{11,1... | collective-permute-start | bytes 3244040 | tf_op jit(solution)/shard_map/ppermute | solution.py:26
  52.0 10.7 %copy-start.4 = (f32[4,16,132,128]{3,2,1,0:T(8,128)}, f32[4,16,132,128]{3,2,1,0:T(8,128)S(1)}, u32[]{:S(2)}) copy-start(f32[4,16,132,128]{3,2,1,0:T(8,128)S(1)} %pad_maximum_fusion.7) | copy-start | bytes 12976132
  52.0 3.1 %copy-start.7 = (f32[2,16,128,128]{3,2,1,0:T(8,128)S(1)}, f32[2,16,128,128]{3,2,1,0:T(8,128)}, u32[]{:S(2)}) copy-start(f32[2,16,128,128]{3,2,1,0:T(8,128)} %copy-done.6) | copy-start | bytes 6291460
  84.3 5.4 %slice-start.2 = ((s8[4456448]{0:T(1024)(128)(4,1)}), s8[4194304]{0:T(1024)(128)(4,1)S(1)}, s32[]{:S(2)}) async-start(s8[4456448]{0:T(1024)(128)(4,1)} %bitcast.77), calls=%async_computation.2 | async-start | bytes 8388608
  84.3 5.4 %slice-start.3 = ((s8[4456448]{0:T(1024)(128)(4,1)}), s8[262144]{0:T(1024)(128)(4,1)S(1)}, s32[]{:S(2)}) async-start(s8[4456448]{0:T(1024)(128)(4,1)} %bitcast.77), calls=%async_computation.3 | async-start | bytes 524288
  91.2 2.5 %copy-start.2 = (f32[4,16,128,128]{3,2,1,0:T(8,128)S(1)}, f32[4,16,128,128]{3,2,1,0:T(8,128)}, u32[]{:S(2)}) copy-start(f32[4,16,128,128]{3,2,1,0:T(8,128)} %param.7) | copy-start | bytes 12582916
  108.5 12.4 %copy-start.10 = (f32[16,130,128]{2,1,0:T(8,128)}, f32[16,130,128]{2,1,0:T(8,128)S(1)}, u32[]{:S(2)}) copy-start(f32[16,130,128]{2,1,0:T(8,128)S(1)} %get-tuple-element.139) | copy-start | bytes 3194884
  108.5 12.4 %copy-start.12 = (f32[16,130,128]{2,1,0:T(8,128)}, f32[16,130,128]{2,1,0:T(8,128)S(1)}, u32[]{:S(2)}) copy-start(f32[16,130,128]{2,1,0:T(8,128)S(1)} %get-tuple-element.140) | copy-start | bytes 3194884
  108.5 12.4 %copy-start.14 = (f32[16,130,128]{2,1,0:T(8,128)}, f32[16,130,128]{2,1,0:T(8,128)S(1)}, u32[]{:S(2)}) copy-start(f32[16,130,128]{2,1,0:T(8,128)S(1)} %get-tuple-element.141) | copy-start | bytes 3194884
  108.5 2.2 copy-start.19
  109.2 17.5 %copy-start.8 = (f32[18,128,128]{2,1,0:T(8,128)}, f32[18,128,128]{2,1,0:T(8,128)S(1)}, u32[]{:S(2)}) copy-start(f32[18,128,128]{2,1,0:T(8,128)S(1)} %get-tuple-element.144) | copy-start | bytes 3538948
  109.2 3.0 %copy-start.17 = (f32[1,18,128,128]{3,2,1,0:T(8,128)S(1)}, f32[1,18,128,128]{3,2,1,0:T(8,128)}, u32[]{:S(2)}) copy-start(f32[1,18,128,128]{3,2,1,0:T(8,128)} %get-tuple-element.44) | copy-start | bytes 3538948
  110.8 10.2 %slice-start = ((s8[4456448]{0:T(1024)(128)(4,1)}), s8[4194304]{0:T(1024)(128)(4,1)S(1)}, s32[]{:S(2)}) async-start(s8[4456448]{0:T(1024)(128)(4,1)} %bitcast.75), calls=%async_computation | async-start | bytes 8388608
  112.2 8.8 %slice-start.1 = ((s8[4456448]{0:T(1024)(128)(4,1)}), s8[262144]{0:T(1024)(128)(4,1)S(1)}, s32[]{:S(2)}) async-start(s8[4456448]{0:T(1024)(128)(4,1)} %bitcast.75), calls=%async_computation.1 | async-start | bytes 524288
  121.0 5.7 %copy-start.16 = (f32[1,18,128,128]{3,2,1,0:T(8,128)S(1)}, f32[1,18,128,128]{3,2,1,0:T(8,128)}, u32[]{:S(2)}) copy-start(f32[1,18,128,128]{3,2,1,0:T(8,128)} %get-tuple-element.83) | copy-start | bytes 3538948
  152.6 11.1 %collective-permute-start.4 = (f32[4,16,2,128]{3,2,1,0:T(2,128)S(1)}, f32[4,16,2,128]{3,2,1,0:T(2,128)S(1)}, u32[]{:S(2)}, u32[]{:S(2)}) collective-permute-start(f32[4,16,2,128]{3,2,1,0:T(2,128)S(1)} %get-tuple-element.119), channel_id=1, source_target_pairs={{0,8},{8,16},{16,24},{24,0},{1,9},{9,17},{17,25},{25,1},{2,10},{10... | collective-permute-start | bytes 196616 | tf_op jit(solution)/shard_map/ppermute | solution.py:23
  152.7 11.0 %copy-start.3 = (f32[4,16,128,128]{3,2,1,0:T(8,128)S(1)}, f32[4,16,128,128]{3,2,1,0:T(8,128)}, u32[]{:S(2)}) copy-start(f32[4,16,128,128]{3,2,1,0:T(8,128)} %fusion.32) | copy-start | bytes 12582916
  152.7 11.0 %collective-permute-start.5 = (f32[4,16,2,128]{3,2,1,0:T(2,128)S(1)}, f32[4,16,2,128]{3,2,1,0:T(2,128)S(1)}, u32[]{:S(2)}, u32[]{:S(2)}) collective-permute-start(f32[4,16,2,128]{3,2,1,0:T(2,128)S(1)} %get-tuple-element.118), channel_id=1, source_target_pairs={{8,0},{16,8},{24,16},{0,24},{9,1},{17,9},{25,17},{1,25},{10,2},{18... | collective-permute-start | bytes 196616 | tf_op jit(solution)/shard_map/ppermute | solution.py:26
  167.3 4.2 %copy-start.18 = (f32[1,16,130,128]{3,2,1,0:T(8,128)S(1)}, f32[1,16,130,128]{3,2,1,0:T(8,128)}, u32[]{:S(2)}) copy-start(f32[1,16,130,128]{3,2,1,0:T(8,128)} %get-tuple-element.10) | copy-start | bytes 3194884
  167.6 12.2 %collective-permute-start.6 = (f32[4,2,132,128]{3,0,2,1:T(4,128)S(1)}, f32[4,2,132,128]{3,0,2,1:T(4,128)S(1)}, u32[]{:S(2)}, u32[]{:S(2)}) collective-permute-start(f32[4,2,132,128]{3,0,2,1:T(4,128)S(1)} %copy.146), channel_id=1, source_target_pairs={{0,1},{1,2},{2,3},{3,4},{4,5},{5,6},{6,7},{7,0},{8,9},{9,10},{10,1... | collective-permute-start | bytes 1622024 | tf_op jit(solution)/shard_map/ppermute | solution.py:23
  168.9 12.2 %collective-permute-start.7 = (f32[4,2,132,128]{3,0,2,1:T(4,128)S(1)}, f32[4,2,132,128]{3,0,2,1:T(4,128)S(1)}, u32[]{:S(2)}, u32[]{:S(2)}) collective-permute-start(f32[4,2,132,128]{3,0,2,1:T(4,128)S(1)} %copy.148), channel_id=1, source_target_pairs={{1,0},{2,1},{3,2},{4,3},{5,4},{6,5},{7,6},{0,7},{9,8},{10,9},{11,1... | collective-permute-start | bytes 1622024 | tf_op jit(solution)/shard_map/ppermute | solution.py:26
  171.5 1.6 copy-start.13
  171.5 1.9 copy-start.15
  (5 other events, 5.8 us)
where the time goes:
time: 230 us; the launch traced here: 227 us
  other arithmetic  132 us (57%)
  local copies, waits for them, and re-layouts  45.9 us (20%)
  blocking collectives  17.8 us (8%)
  starting transfers between devices  13.1 us (6%)
  waiting for transfers between devices  10.3 us (4%)
  between operations  7.9 us (3%)
    div x1, other arithmetic, per_device(): (volume_old * flow_state - SECTION_WEIGHTS[1] * TIME_STEP * residual(padd...  34.6 us
    div x1, other arithmetic, per_device(): (volume_old * flow_state - SECTION_WEIGHTS[0] * TIME_STEP * residual(padd...  21.3 us
    psum x1, blocking collectives, broadcast(): return lax.psum(jnp.where(mine, value, jnp.zeros_like(value)), axis)  17.8 us
    slice x2, local copies, waits for them, and re-layouts, radial_damping(): last_row = lax.slice_in_dim(values, count - 1, count, axis=axis_pos)  16.3 us
    sub x4, other arithmetic, directional(): return first_coef * flux_x + second_coef * flux_y - sweep_term * strip_cells  15.4 us
    ppermute x4, starting transfers between devices, padded_2(): lax.ppermute(lax.slice_in_dim(block, 0, width, axis=dim), axis, backward)  12 us
    concatenate x4, other arithmetic, finish_flow(): return jnp.concatenate([top_rows, whole[:, depth:-depth], bottom_rows], 1)  10.3 us
    concatenate x2, other arithmetic, fill_ends(): jnp.concatenate([low_side, lax.slice_in_dim(padded, depth, length - depth...  9.98 us
  transfers between devices with their start and end apart: 8, of which 3 were waited for; matrix products, arithmetic and copies ran while one was open for 16% of the time, Pallas kernels for 0%

commit v1 on v0

v1 whole, which is shorter than its diff:
```python
import functools

import jax
import jax.numpy as jnp
from jax import lax
from jax.experimental import pallas as pl
from jax.experimental.pallas import tpu as pltpu
from jax.sharding import PartitionSpec as P

MESH = pl.DeviceIdType.MESH
F32 = jnp.float32
TIME_STEP = 0.25
DAMPING = 0.02
SECTION_WEIGHTS = (0.5, 1.0)
PAD = 8
CHUNK = 16


def kernel(
    n_pitch, n_span, AL, PL, R, HARM,
    phase, flow_hbm, node_hbm, mode, lag,
    state_out, moved_out,
    S0, S1, N, M, GE, H, G, RAD, W, MODE, CORR, TRIG, SB0, RB0, SB1, RB1, CS, CR,
    loc, send, recv, wsend, wrecv, osem,
):
    me_p = lax.axis_index("pitch")
    me_s = lax.axis_index("span")
    left = lax.rem(me_p + n_pitch - 1, n_pitch)
    right = lax.rem(me_p + 1, n_pitch)
    low_end = me_p == 0
    high_end = me_p == n_pitch - 1
    first = me_s == 0
    last = me_s == n_span - 1
    not_first = me_s > 0
    not_last = me_s < n_span - 1
    total_pitch = PL * n_pitch
    total_axial = AL * n_span
    lead = total_axial // 4
    lo, hi = PAD, PAD + PL
    def by_rows(count, body, step):
        def several(i, _):
            for j in range(step):
                body(i * step + j, 0)
            return 0

        lax.fori_loop(0, count // step, several, 0)

    def remote(src, dst, number, p, s):
        return pltpu.make_async_remote_copy(
            src_ref=src, dst_ref=dst, send_sem=send.at[number], recv_sem=recv.at[number],
            device_id=(p, s), device_id_type=MESH,
        )

    node_in = pltpu.make_async_copy(
        node_hbm, N.at[:, pl.ds(1, AL), pl.ds(lo, PL), :], loc.at[0]
    )
    flow_in = pltpu.make_async_copy(
        flow_hbm, S0.at[:, pl.ds(2, AL), pl.ds(lo, PL), :], loc.at[1]
    )
    node_in.start()
    flow_in.start()

    above = lax.rem(me_s + n_span - 1, n_span)
    below = lax.rem(me_s + 1, n_span)

    barrier = pltpu.get_barrier_semaphore()
    for step in range(1, n_pitch):
        other = lax.rem(me_p + step, n_pitch)
        pl.semaphore_signal(barrier, inc=1, device_id=(other, me_s), device_id_type=MESH)

    @pl.when(not_first)
    def _():
        for other in range(n_pitch):
            pl.semaphore_signal(
                barrier, inc=1, device_id=(other, above), device_id_type=MESH
            )

    @pl.when(not_last)
    def _():
        for other in range(n_pitch):
            pl.semaphore_signal(
                barrier, inc=1, device_id=(other, below), device_id_type=MESH
            )

    rows = lax.broadcasted_iota(jnp.int32, (16, R), 0)
    harmonic = jnp.where(rows < 2, 0, lax.rem(rows + 1, 3)) + 1
    move = jnp.where(rows == 1, 1, jnp.where(rows < 2, 0, jnp.where(rows < 5, -1, jnp.where(rows < 8, 0, 1))))
    now = phase[0]
    lagging = phase[1]
    angle = harmonic.astype(F32) * (now + move.astype(F32) * lagging)
    TRIG[0] = jnp.cos(angle)
    TRIG[1] = jnp.sin(angle)

    def trig(kind, row):
        return TRIG[kind, row:row + 1, :]

    for side, base in ((0, 2), (1, 8)):
        series = 1 - side
        for var in range(4):
            total = None
            for k in range(HARM):
                change_cos = trig(0, base + k) - trig(0, 5 + k)
                change_sin = trig(1, base + k) - trig(1, 5 + k)
                term = lag[series, k, 0, var] * change_cos - lag[series, k, 1, var] * change_sin
                total = term if total is None else total + term
            for a in range(AL):
                CORR[side, var, a] = total[a:a + 1, :]
    for part in range(2):
        for a in range(AL):
            MODE[part, a] = mode[part, a:a + 1, :]

    def blade_at(a):
        at = me_s * AL + a
        return (at >= lead) & (at < total_axial - lead)

    node_in.wait()

    def wall_rows(side, early, late):
        def body(a, _):
            nx = N[0, a + 1, late:late + 1, :] - N[0, a + 1, early:early + 1, :]
            ny = 1.0 + N[1, a + 1, late:late + 1, :] - N[1, a + 1, early:early + 1, :]
            length = jnp.sqrt(nx * nx + ny * ny)
            amp = MODE[0, a] * trig(0, side) - MODE[1, a] * trig(1, side)
            amp = jnp.where(blade_at(a), amp, 0.0)
            W[side, 0, a + 1] = amp * (nx / length)
            W[side, 1, a + 1] = amp * (ny / length)
            return 0

        by_rows(AL, body, 8)

    @pl.when(low_end)
    def _():
        wall_rows(0, lo, lo + 1)

    @pl.when(high_end)
    def _():
        wall_rows(1, hi - 2, hi - 1)

    for left_row, src in ((0, hi - 1), (1, lo)):
        for end, a in ((0, AL), (1, 1)):
            number = 2 * end + left_row
            CS[number] = N[:, a, src:src + 1, :]

    sides = jnp.where(not_first, 1, 0) + jnp.where(not_last, 1, 0)
    pl.semaphore_wait(barrier, n_pitch - 1 + n_pitch * sides)

    def wall_copy(side, kind, p, s, step):
        src, dst = ((1, 1), (1, AL + 1), (AL, 0))[kind]
        size = AL if kind == 0 else 1
        return pltpu.make_async_remote_copy(
            src_ref=W.at[side, :, pl.ds(src, size)],
            dst_ref=W.at[side, :, pl.ds(dst, size)],
            send_sem=wsend.at[(side * 3 + kind) * n_pitch + step],
            recv_sem=wrecv.at[side * 3 + kind],
            device_id=(p, s), device_id_type=MESH,
        )

    def walls(act):
        for side, own in ((0, low_end), (1, high_end)):
            @pl.when(own)
            def _(side=side):
                for step in range(1, n_pitch):
                    act(wall_copy(side, 0, lax.rem(me_p + step, n_pitch), me_s, step))

                @pl.when(not_first)
                def _():
                    for other in range(n_pitch):
                        act(wall_copy(side, 1, other, above, other))

                @pl.when(not_last)
                def _():
                    for other in range(n_pitch):
                        act(wall_copy(side, 2, other, below, other))

    walls(lambda copy: copy.start())

    field = pl.ds(lo, PL)
    node_up = remote(node_hbm.at[:, pl.ds(0, 1)], N.at[:, pl.ds(AL + 1, 1), field], 0, me_p, above)
    node_down = remote(node_hbm.at[:, pl.ds(AL - 1, 1)], N.at[:, pl.ds(0, 1), field], 1, me_p, below)
    flow_up = remote(flow_hbm.at[:, pl.ds(0, 2)], S0.at[:, pl.ds(AL + 2, 2), field], 2, me_p, above)
    flow_down = remote(flow_hbm.at[:, pl.ds(AL - 2, 2)], S0.at[:, pl.ds(0, 2), field], 3, me_p, below)
    to_left = remote(SB0.at[0], RB0.at[1], 4, left, me_s)
    to_right = remote(SB0.at[1], RB0.at[0], 5, right, me_s)
    corner_down = [
        remote(CS.at[0], CR.at[0], 6, right, below),
        remote(CS.at[1], CR.at[1], 7, left, below),
    ]
    corner_up = [
        remote(CS.at[2], CR.at[2], 8, right, above),
        remote(CS.at[3], CR.at[3], 9, left, above),
    ]
    next_up = remote(S1.at[:, pl.ds(2, 2), field], S1.at[:, pl.ds(AL + 2, 2), field], 10, me_p, above)
    next_down = remote(S1.at[:, pl.ds(AL, 2), field], S1.at[:, pl.ds(0, 2), field], 11, me_p, below)
    next_left = remote(SB1.at[0], RB1.at[1], 12, left, me_s)
    next_right = remote(SB1.at[1], RB1.at[0], 13, right, me_s)

    @pl.when(not_first)
    def _():
        node_up.start()
        for copy in corner_up:
            copy.start()
        flow_up.start()

    @pl.when(not_last)
    def _():
        node_down.start()
        for copy in corner_down:
            copy.start()
        flow_down.start()

    flow_in.wait()

    def pack(S, B):
        def body(a, _):
            for var in range(4):
                B[0, var, a] = S[var, a + 2, lo:lo + 2, :]
                B[1, var, a] = S[var, a + 2, hi - 2:hi, :]
            return 0

        by_rows(AL, body, 4)

    def pack_node(a, _):
        for var in range(2):
            SB0[0, 4 + var, a] = N[var, a + 1, lo:lo + 2, :]
            SB0[1, 4 + var, a] = N[var, a + 1, hi - 2:hi, :]
        return 0

    pack(S0, SB0)
    by_rows(AL, pack_node, 4)
    to_left.start()
    to_right.start()

    to_left.wait_recv()
    to_right.wait_recv()

    def node_edges(a, _):
        for var in range(2):
            N[var, a + 1, lo - 1:lo, :] = RB0[0, 4 + var, a, 1:2, :]
            N[var, a + 1, hi:hi + 1, :] = RB0[1, 4 + var, a, 0:1, :]
        return 0

    by_rows(AL, node_edges, 4)

    @pl.when(not_first)
    def _():
        node_down.wait_recv()
        for copy in corner_down:
            copy.wait_recv()
        N[:, 0, lo - 1:lo, :] = CR[0]
        N[:, 0, hi:hi + 1, :] = CR[1]

    @pl.when(not_last)
    def _():
        node_up.wait_recv()
        for copy in corner_up:
            copy.wait_recv()
        N[:, AL + 1, lo - 1:lo, :] = CR[2]
        N[:, AL + 1, hi:hi + 1, :] = CR[3]

    @pl.when(first)
    def _():
        for var in range(2):
            N[var, 0] = 2.0 * N[var, 1] - N[var, 2]

    @pl.when(last)
    def _():
        for var in range(2):
            N[var, AL + 1] = 2.0 * N[var, AL] - N[var, AL - 1]

    @pl.when(low_end)
    def _():
        def body(a, _):
            for var in range(2):
                N[var, a, lo - 1:lo, :] = 2.0 * N[var, a, lo:lo + 1, :] - N[var, a, lo + 1:lo + 2, :]
            return 0

        lax.fori_loop(0, AL + 2, body, 0)

    @pl.when(high_end)
    def _():
        def body(a, _):
            for var in range(2):
                N[var, a, hi:hi + 1, :] = 2.0 * N[var, a, hi - 1:hi, :] - N[var, a, hi - 2:hi - 1, :]
            return 0

        lax.fori_loop(0, AL + 2, body, 0)

    low_gate = jnp.where(low_end, 1.0, 0.0)
    high_gate = jnp.where(high_end, 1.0, 0.0)

    def pitch_edges(S, B):
        def body(a, _):
            blade = blade_at(a)
            low_wall = blade & low_end
            high_wall = blade & high_end
            for var in range(4):
                sign = -1.0 if var == 2 else 1.0
                low_corr = CORR[0, var, a] * low_gate
                high_corr = CORR[1, var, a] * high_gate
                for row in range(2):
                    mirror = S[var, a + 2, lo + 1 - row:lo + 2 - row, :] * sign
                    arrived = B[0, var, a, row:row + 1, :] + low_corr
                    S[var, a + 2, lo - 2 + row:lo - 1 + row, :] = jnp.where(low_wall, mirror, arrived)
                    mirror = S[var, a + 2, hi - 1 - row:hi - row, :] * sign
                    arrived = B[1, var, a, row:row + 1, :] + high_corr
                    S[var, a + 2, hi + row:hi + row + 1, :] = jnp.where(high_wall, mirror, arrived)
            return 0

        by_rows(AL, body, 4)

    inner = [(q, CHUNK) for q in range(lo, hi, CHUNK)]
    outer = [(0, PAD), (hi, PAD)]

    def along_pitch(T, a, q, size):
        return [
            T[comp, a, q + 1:q + 1 + size, :] - T[comp, a, q - 1:q - 1 + size, :] for comp in range(2)
        ]

    def along_axis(T, a, q, size):
        return [T[comp, a + 1, q:q + size, :] - T[comp, a - 1, q:q + size, :] for comp in range(2)]

    def old_row(i, _):
        a = i + 1
        for q, size in inner:
            px, py = along_pitch(N, a, q, size)
            zx, zy = along_axis(N, a, q, size)
            GE[6, a, q:q + size, :] = (2.0 + zx) * (2.0 + py) - px * zy
        return 0

    pitch_edges(S0, RB0)
    lax.fori_loop(0, AL, old_row, 0)

    for side, own in ((0, low_end), (1, high_end)):
        @pl.when(jnp.logical_not(own))
        def _(side=side):
            wall_copy(side, 0, me_p, me_s, 0).wait_recv()

        @pl.when(not_last)
        def _(side=side):
            wall_copy(side, 1, me_p, me_s, 0).wait_recv()

        @pl.when(not_first)
        def _(side=side):
            wall_copy(side, 2, me_p, me_s, 0).wait_recv()

        @pl.when(first)
        def _(side=side):
            W[side, :, 0] = 2.0 * W[side, :, 1] - W[side, :, 2]

        @pl.when(last)
        def _(side=side):
            W[side, :, AL + 1] = 2.0 * W[side, :, AL] - W[side, :, AL - 1]

    def shift_of(a, q, size):
        at = me_p * PL + (q - lo) + lax.broadcasted_iota(jnp.int32, (size, R), 0)
        blend = at.astype(F32) * (1.0 / (total_pitch - 1))
        out = []
        for comp in range(2):
            low = W[0, comp, a]
            out.append(low + blend * (W[1, comp, a] - low))
        return out

    def move_row(a, _):
        for q, size in outer + inner:
            for comp, shift in enumerate(shift_of(a, q, size)):
                M[comp, a, q:q + size, :] = N[comp, a, q:q + size, :] + shift
        return 0

    lax.fori_loop(0, AL + 2, move_row, 0)
    moved_copy = pltpu.make_async_copy(M.at[:, pl.ds(1, AL), field], moved_out, osem.at[0])
    moved_copy.start()

    def axial_terms(a, q, size):
        px, py = along_pitch(M, a, q, size)
        c, e = 2.0 + py, -px
        sx, sy = shift_of(a, q, size)
        GE[3, a, q:q + size, :] = c
        GE[4, a, q:q + size, :] = e
        GE[5, a, q:q + size, :] = (c * sx + e * sy) * (1.0 / TIME_STEP)
        return c, e

    def pitch_terms(a, q, size):
        zx, zy = along_axis(M, a, q, size)
        first_c, second_c = -zy, 2.0 + zx
        sx, sy = shift_of(a, q, size)
        GE[0, a, q:q + size, :] = first_c
        GE[1, a, q:q + size, :] = second_c
        GE[2, a, q:q + size, :] = (first_c * sx + second_c * sy) * (1.0 / TIME_STEP)
        return first_c, second_c

    def metric_row(i, _):
        a = i + 1
        for q, size in outer:
            pitch_terms(a, q, size)
        for q, size in inner:
            c, e = axial_terms(a, q, size)
            first_c, second_c = pitch_terms(a, q, size)
            new = second_c * c - e * first_c
            inverse = 1.0 / new
            GE[6, a, q:q + size, :] = GE[6, a, q:q + size, :] * inverse
            GE[7, a, q:q + size, :] = TIME_STEP * inverse
        return 0

    for a in (0, AL + 1):
        for q, size in inner:
            axial_terms(a, q, size)
    lax.fori_loop(0, AL, metric_row, 0)

    def flux(S, a, q, size, pitch, axial):
        r, mx, my, e = [S[var, a + 1, q:q + size, :] for var in range(4)]
        guess = pl.reciprocal(r, approx=True)
        inverse = guess * (2.0 - r * guess)
        u = mx * inverse
        v = my * inverse
        p = 0.4 * e - 0.2 * (mx * u + my * v)
        done = []
        for wanted, base in ((pitch, 0), (axial, 3)):
            if not wanted:
                done.append(None)
                continue
            c0, c1, sweep = [GE[base + j, a, q:q + size, :] for j in range(3)]
            w = c0 * u + c1 * v
            rel = w - sweep
            done.append((r * rel, mx * rel + c0 * p, my * rel + c1 * p, e * rel + p * w))
        return done

    def flux_field(S):
        def body(i, _):
            a = i + 1
            for q, size in inner:
                pitch_flux, axial_flux = flux(S, a, q, size, True, True)
                for var in range(4):
                    G[var, i, q:q + size, :] = pitch_flux[var]
                    H[var, a, q - lo:q - lo + size, :] = axial_flux[var]
            return 0

        lax.fori_loop(0, AL, body, 0)

    def flux_sides(S):
        def body(i, _):
            for q, size in outer:
                pitch_flux, _unused = flux(S, i + 1, q, size, True, False)
                for var in range(4):
                    G[var, i, q:q + size, :] = pitch_flux[var]
            return 0

        lax.fori_loop(0, AL, body, 0)

    def flux_ends(S):
        for a in (0, AL + 1):
            for q, size in inner:
                _unused, axial_flux = flux(S, a, q, size, False, True)
                for var in range(4):
                    H[var, a, q - lo:q - lo + size, :] = axial_flux[var]

    at_row = lax.broadcasted_iota(jnp.int32, (R, R), 0)
    at_col = lax.broadcasted_iota(jnp.int32, (R, R), 1)
    radial = jnp.zeros((R, R), F32)
    for offset, weight in ((-2, 1.0), (-1, -4.0), (0, 6.0), (1, -4.0), (2, 1.0)):
        source = jnp.clip(at_col + offset, 0, R - 1)
        radial = radial + jnp.where(at_row == source, weight, 0.0)
    radial = jnp.concatenate([radial, radial], axis=0).astype(jnp.bfloat16)

    def residual_row(S, i, weight, put):
        a = i + 2
        for var in range(4):
            values = S[var, a, lo:hi, :]
            head = values.astype(jnp.bfloat16)
            tail = (values - head.astype(F32)).astype(jnp.bfloat16)
            RAD[var] = jnp.dot(
                jnp.concatenate([head, tail], axis=1), radial, preferred_element_type=F32
            )
        for q, size in inner:
            keep = GE[6, i + 1, q:q + size, :]
            rate = GE[7, i + 1, q:q + size, :] * weight
            h = q - lo
            for var in range(4):
                here = S[var, a, q:q + size, :]
                near = (S[var, a, q + 1:q + 1 + size, :] + S[var, a, q - 1:q - 1 + size, :]) + (
                    S[var, a + 1, q:q + size, :] + S[var, a - 1, q:q + size, :]
                )
                far = (S[var, a, q + 2:q + 2 + size, :] + S[var, a, q - 2:q - 2 + size, :]) + (
                    S[var, a + 2, q:q + size, :] + S[var, a - 2, q:q + size, :]
                )
                fourth = (far + RAD[var, h:h + size, :]) + (12.0 * here - 4.0 * near)
                change = (G[var, i, q + 1:q + 1 + size, :] - G[var, i, q - 1:q - 1 + size, :]) + (
                    H[var, i + 2, h:h + size, :] - H[var, i, h:h + size, :]
                )
                value = keep * S0[var, a, q:q + size, :] - rate * (change + (4.0 * DAMPING) * fourth)
                put(var, i, q, size, value)

    def put_one(var, i, q, size, value):
        S1[var, i + 2, q:q + size, :] = value

    def put_two(var, i, q, size, value):
        S0[var, i + 2, q:q + size, :] = value

    def residual_inner(S, weight, put):
        def body(i, _):
            residual_row(S, i + 2, weight, put)
            return 0

        lax.fori_loop(0, AL - 4, body, 0)

    def residual_ends(S, weight, put):
        def body(i, _):
            residual_row(S, i + (AL - 4) * (i // 2), weight, put)
            return 0

        lax.fori_loop(0, 4, body, 0)

    def axial_edges(S, down, up):
        @pl.when(not_first)
        def _():
            down.wait_recv()

        @pl.when(not_last)
        def _():
            up.wait_recv()

        @pl.when(first)
        def _():
            for var in range(4):
                row = S[var, 2, lo:hi, :]
                S[var, 0, lo:hi, :] = row
                S[var, 1, lo:hi, :] = row

        @pl.when(last)
        def _():
            for var in range(4):
                row = S[var, AL + 1, lo:hi, :]
                S[var, AL + 2, lo:hi, :] = row
                S[var, AL + 3, lo:hi, :] = row

    flux_field(S0)
    flux_sides(S0)
    residual_inner(S0, SECTION_WEIGHTS[0], put_one)
    axial_edges(S0, flow_down, flow_up)
    flux_ends(S0)
    residual_ends(S0, SECTION_WEIGHTS[0], put_one)

    @pl.when(not_first)
    def _():
        next_up.start()

    @pl.when(not_last)
    def _():
        next_down.start()

    pack(S1, SB1)
    next_left.start()
    next_right.start()

    flux_field(S1)
    next_left.wait_recv()
    next_right.wait_recv()
    pitch_edges(S1, RB1)
    flux_sides(S1)
    residual_inner(S1, SECTION_WEIGHTS[1], put_two)
    out_inner = pltpu.make_async_copy(
        S0.at[:, pl.ds(4, AL - 4), field], state_out.at[:, pl.ds(2, AL - 4)], osem.at[1]
    )
    out_inner.start()
    axial_edges(S1, next_down, next_up)
    flux_ends(S1)
    residual_ends(S1, SECTION_WEIGHTS[1], put_two)
    out_first = pltpu.make_async_copy(
        S0.at[:, pl.ds(2, 2), field], state_out.at[:, pl.ds(0, 2)], osem.at[2]
    )
    out_last = pltpu.make_async_copy(
        S0.at[:, pl.ds(AL, 2), field], state_out.at[:, pl.ds(AL - 2, 2)], osem.at[3]
    )
    out_first.start()
    out_last.start()

    walls(lambda copy: copy.wait_send())

    @pl.when(not_first)
    def _():
        for copy in [node_up, flow_up, next_up] + corner_up:
            copy.wait_send()

    @pl.when(not_last)
    def _():
        for copy in [node_down, flow_down, next_down] + corner_down:
            copy.wait_send()

    for copy in (to_left, to_right, next_left, next_right):
        copy.wait_send()
    moved_copy.wait()
    out_inner.wait()
    out_first.wait()
    out_last.wait()


def solution(mesh):
    n_pitch = mesh.shape["pitch"]
    n_span = mesh.shape["span"]

    def per_device(flow_state, node_offset, blade_mode, phase_angles, lag_series):
        _, AL, PL, R = flow_state.shape
        HARM = lag_series.shape[1]
        width = PL + 2 * PAD
        vmem = lambda *shape: pltpu.VMEM(shape, F32)
        dma = lambda count: pltpu.SemaphoreType.DMA((count,))
        return pl.pallas_call(
            functools.partial(kernel, n_pitch, n_span, AL, PL, R, HARM),
            out_shape=(
                jax.ShapeDtypeStruct(flow_state.shape, F32),
                jax.ShapeDtypeStruct(node_offset.shape, F32),
            ),
            in_specs=[
                pl.BlockSpec(memory_space=pltpu.SMEM),
                pl.BlockSpec(memory_space=pl.ANY),
                pl.BlockSpec(memory_space=pl.ANY),
                pl.BlockSpec(memory_space=pltpu.VMEM),
                pl.BlockSpec(memory_space=pltpu.VMEM),
            ],
            out_specs=(pl.BlockSpec(memory_space=pl.ANY), pl.BlockSpec(memory_space=pl.ANY)),
            scratch_shapes=[
                vmem(4, AL + 4, width, R),
                vmem(4, AL + 4, width, R),
                vmem(2, AL + 2, width, R),
                vmem(2, AL + 2, width, R),
                vmem(8, AL + 2, width, R),
                vmem(4, AL + 2, PL, R),
                vmem(4, AL, width, R),
                vmem(4, PL, R),
                vmem(2, 2, AL + 2, 1, R),
                vmem(2, AL, 1, R),
                vmem(2, 4, AL, 1, R),
                vmem(2, 16, R),
                vmem(2, 6, AL, 2, R),
                vmem(2, 6, AL, 2, R),
                vmem(2, 4, AL, 2, R),
                vmem(2, 4, AL, 2, R),
                vmem(4, 2, 1, R),
                vmem(4, 2, 1, R),
                dma(2), dma(14), dma(14), dma(6 * n_pitch), dma(6), dma(4),
            ],
            compiler_params=pltpu.CompilerParams(
                collective_id=0, has_side_effects=True, vmem_limit_bytes=56 * 2**20
            ),
        )(phase_angles, flow_state, node_offset, blade_mode, lag_series)

    placed = (
        P(None, "span", "pitch", None),
        P(None, "span", "pitch", None),
        P(None, "span", None),
        P(),
        P(None, None, None, None, "span", None),
    )
    return jax.shard_map(
        per_device,
        mesh=mesh,
        in_specs=placed,
        out_specs=(P(None, "span", "pitch", None), P(None, "span", "pitch", None)),
        check_vma=False,
    )
```

time: 230 us -> 41.1 us (0.18); the launches traced: 227 us -> 41 us
  other arithmetic: 132 us -> 0 us
  local copies, waits for them, and re-layouts: 45.9 us -> 6.17 us
  Pallas kernels: 0 us -> 34.1 us
  blocking collectives: 17.8 us -> 0 us
  starting transfers between devices: 13.1 us -> 0 us
  waiting for transfers between devices: 10.3 us -> 0 us
  between operations: 7.9 us -> 0.65 us
    div x7 -> x0, other arithmetic: 56.2 us -> none  [the longest x1 34.6 us: per_device(): (volume_old * flow_state - SECTION_WEIGHTS[1] * TIME_STEP * residual(padd...]
    slice x16 -> x0, local copies, waits for them, and re-layouts: 37 us -> none  [the longest x2 16.3 us: radial_damping(): last_row = lax.slice_in_dim(values, count - 1, count, axis=axis_pos)]
    pallas_call x0 -> x1, Pallas kernels: none -> 34.1 us  [per_device(): pl.pallas_call(functools.partial(kernel, n_pitch, n_span, AL, PL, R, HARM...]
    concatenate x10 -> x0, other arithmetic: 23.7 us -> none  [the longest x4 10.3 us: finish_flow(): return jnp.concatenate([top_rows, whole[:, depth:-depth], bottom_rows], 1)]
    sub x9 -> x0, other arithmetic: 22.7 us -> none  [the longest x4 15.4 us: directional(): return first_coef * flux_x + second_coef * flux_y - sweep_term * strip_cells]
    add x13 -> x0, other arithmetic: 18.5 us -> none  [the longest x4 7.27 us: directional(): strip_cells[2] * vel_y + pressure]
    psum x1 -> x0, blocking collectives: 17.8 us -> none  [broadcast(): return lax.psum(jnp.where(mine, value, jnp.zeros_like(value)), axis)]
    ppermute x8 -> x0, starting transfers between devices: 13.1 us -> none  [the longest x4 12 us: padded_2(): lax.ppermute(lax.slice_in_dim(block, 0, width, axis=dim), axis, backward)]
  transfers between devices with their start and end apart: 8 -> 0, of which waited for: 3 -> 0; matrix products, arithmetic and copies ran while one was open for 16% -> 0% of each run, Pallas kernels for 0% -> 0%
where the time goes in v1:
time: 41.1 us; the launch traced here: 41 us
  Pallas kernels  34.1 us (83%)
  local copies, waits for them, and re-layouts  6.17 us (15%)
  between operations  0.65 us (2%)
    pallas_call x1, Pallas kernels, per_device(): pl.pallas_call(functools.partial(kernel, n_pitch, n_span, AL, PL, R, HARM...  34.1 us
    unnamed x4, local copies, waits for them, and re-layouts  6.17 us

profile of v1, /device:TPU:0, one launch (start us, length us, event | category | flops | bytes accessed | tf_op | source)
XLA Modules:
  0.0 41.0 jit_solution(1985599368544048699)
XLA Ops:
  0.6 34.1 %shard_map.68 = (f32[4,16,128,128]{3,2,1,0:T(8,128)}, f32[2,16,128,128]{3,2,1,0:T(8,128)}) custom-call(f32[2]{0:T(128)} %phase.1, f32[4,16,128,128]{3,2,1,0:T(8,128)} %flow_hbm.1, f32[2,16,128,128]{3,2,1,0:T(8,128)} %node_hbm.1, f32[2,16,128]{2,1,0:T(8,128)} %mode.1, f32[2,3,2,4,16,128]{5,4,3,2,1,0:T(8,128)} %lag.1), custom_call_target="tpu_custom_call" | custom-call | tf_op jit(solution)/shard_map/pallas_call | solution.py:606
  34.8 0.0 copy-start
  34.8 4.8 %copy.9 = f32[4,16,128,128]{3,2,1,0:T(8,128)} copy(f32[4,16,128,128]{3,2,1,0:T(8,128)} %get-tuple-element.4) | data formatting | bytes 8388608
  39.6 0.0 copy-done
  39.6 1.3 %copy.10 = f32[2,16,128,128]{3,2,1,0:T(8,128)} copy(f32[2,16,128,128]{3,2,1,0:T(8,128)S(1)} %copy-done) | data formatting | bytes 4194304
Async XLA Ops:
  34.8 4.9 %copy-start = (f32[2,16,128,128]{3,2,1,0:T(8,128)S(1)}, f32[2,16,128,128]{3,2,1,0:T(8,128)}, u32[]{:S(2)}) copy-start(f32[2,16,128,128]{3,2,1,0:T(8,128)} %get-tuple-element.5) | copy-start | bytes 6291460

commit v2 on v1

--- a/solution.py
+++ b/solution.py
@@ -639,7 +639,7 @@
                 dma(2), dma(14), dma(14), dma(6 * n_pitch), dma(6), dma(4),
             ],
             compiler_params=pltpu.CompilerParams(
-                collective_id=0, has_side_effects=True, vmem_limit_bytes=56 * 2**20
+                collective_id=0, has_side_effects=True, vmem_limit_bytes=44 * 2**20
             ),
         )(phase_angles, flow_state, node_offset, blade_mode, lag_series)
 

time: 41.1 us -> 42.1 us (1.024)
  local copies, waits for them, and re-layouts: 6.17 us -> 7.29 us
    unnamed x4 -> x10, local copies, waits for them, and re-layouts: 6.17 us -> 7.29 us
where the time goes in v2:
time: 42.1 us; the launch traced here: 41.9 us
  Pallas kernels  33.9 us (81%)
  local copies, waits for them, and re-layouts  7.29 us (17%)
  between operations  0.65 us (2%)
    pallas_call x1, Pallas kernels, per_device(): pl.pallas_call(functools.partial(kernel, n_pitch, n_span, AL, PL, R, HARM...  33.9 us
    unnamed x10, local copies, waits for them, and re-layouts  7.29 us

profile of v2, /device:TPU:0, one launch (start us, length us, event | category | flops | bytes accessed | tf_op | source)
XLA Modules:
  0.0 41.9 jit_solution(4354974902721916153)
XLA Ops:
  0.6 0.0 copy-start
  0.6 1.6 %copy-done = f32[2,16,128,128]{3,2,1,0:T(8,128)S(1)} copy-done((f32[2,16,128,128]{3,2,1,0:T(8,128)S(1)}, f32[2,16,128,128]{3,2,1,0:T(8,128)}, u32[]{:S(2)}) %copy-start) | copy-done | bytes 2097176
  2.2 0.0 copy-start.1
  2.2 1.0 %copy-done.1 = f32[2,3,2,4,16,128]{5,4,3,2,1,0:T(8,128)S(1)} copy-done((f32[2,3,2,4,16,128]{5,4,3,2,1,0:T(8,128)S(1)}, f32[2,3,2,4,16,128]{5,4,3,2,1,0:T(8,128)}, u32[]{:S(2)}) %copy-start.1) | copy-done | bytes 393240
  3.2 0.0 copy-start.2
  3.2 0.7 %copy-done.2 = f32[2,16,128]{2,1,0:T(8,128)S(1)} copy-done((f32[2,16,128]{2,1,0:T(8,128)S(1)}, f32[2,16,128]{2,1,0:T(8,128)}, u32[]{:S(2)}) %copy-start.2) | copy-done | bytes 16408
  3.9 0.0 copy-start.3
  3.9 0.7 %copy-done.3 = f32[2]{0:T(128)S(1)} copy-done((f32[2]{0:T(128)S(1)}, f32[2]{0:T(128)}, u32[]{:S(2)}) %copy-start.3) | copy-done | bytes 32
  4.6 33.9 %shard_map.68 = (f32[4,16,128,128]{3,2,1,0:T(8,128)S(1)}, f32[2,16,128,128]{3,2,1,0:T(8,128)S(1)}) custom-call(f32[2]{0:T(128)S(1)} %copy-done.3, f32[4,16,128,128]{3,2,1,0:T(8,128)} %flow_hbm.1, f32[2,16,128,128]{3,2,1,0:T(8,128)S(1)} %copy-done, f32[2,16,128]{2,1,0:T(8,128)S(1)} %copy-done.2, f32[2,3,2,4,16,128]{5,4,3,2,1,0:T(8,128)S(1)} %copy-done.1), custom_call_target="tpu_custom_call" | custom-call | tf_op jit(solution)/shard_map/pallas_call | solution.py:606
  38.5 2.0 %copy.9 = f32[4,16,128,128]{3,2,1,0:T(8,128)} copy(f32[4,16,128,128]{3,2,1,0:T(8,128)S(1)} %get-tuple-element.4) | data formatting | bytes 8388608
  40.5 1.3 %copy.10 = f32[2,16,128,128]{3,2,1,0:T(8,128)} copy(f32[2,16,128,128]{3,2,1,0:T(8,128)S(1)} %get-tuple-element.5) | data formatting | bytes 4194304
Async XLA Ops:
  0.6 1.6 %copy-start = (f32[2,16,128,128]{3,2,1,0:T(8,128)S(1)}, f32[2,16,128,128]{3,2,1,0:T(8,128)}, u32[]{:S(2)}) copy-start(f32[2,16,128,128]{3,2,1,0:T(8,128)} %node_hbm.1) | copy-start | bytes 6291460
  2.2 1.0 %copy-start.1 = (f32[2,3,2,4,16,128]{5,4,3,2,1,0:T(8,128)S(1)}, f32[2,3,2,4,16,128]{5,4,3,2,1,0:T(8,128)}, u32[]{:S(2)}) copy-start(f32[2,3,2,4,16,128]{5,4,3,2,1,0:T(8,128)} %lag.1) | copy-start | bytes 1179652
  3.2 0.7 %copy-start.2 = (f32[2,16,128]{2,1,0:T(8,128)S(1)}, f32[2,16,128]{2,1,0:T(8,128)}, u32[]{:S(2)}) copy-start(f32[2,16,128]{2,1,0:T(8,128)} %mode.1) | copy-start | bytes 49156
  3.9 0.7 %copy-start.3 = (f32[2]{0:T(128)S(1)}, f32[2]{0:T(128)}, u32[]{:S(2)}) copy-start(f32[2]{0:T(128)} %phase.1) | copy-start | bytes 28
